TPU v7x, 32 devices: a whole 2x2x4 slice. The times are simulated.
32 devices in a mesh: groups: 1, epouter: 16 (over z, y, core), epinner: 2 (over x).
Axes of the slice: x: 2, y: 2, z: 4, core: 2. Of those that a mesh axis runs over, the one named last changes fastest.
Arguments:
- tokens: bfloat16 [1024, 7168], P(('groups', 'epouter'), 'epinner'), may hold values from -6 to 6
- expert_ids: int32 [1024, 2], P(('groups', 'epouter')), may hold values from 0 to 3, all different within a row; in each aligned block of 64 rows (0 to 63, 64 to 127, ...) at most 48 rows name the same one
- route_weight: float32 [1024, 2], P(('groups', 'epouter')), may hold values from 0.1 to 0.5
- w_gate: bfloat16 [16, 7168, 384], P('epouter', 'epinner'), may hold values from -0.0625 to 0.0625
- w_up: bfloat16 [16, 7168, 384], P('epouter', 'epinner'), may hold values from -0.0625 to 0.0625
- w_down: bfloat16 [16, 384, 7168], P('epouter', None, 'epinner'), may hold values from -0.15625 to 0.15625
Outputs:
- moe_out: bfloat16 [1024, 7168], P(('groups', 'epouter'), 'epinner')
Inputs may be any that keep to these rules, and one draw needn't show every extreme that they name: `expert_ids`: each row names 2 different experts; in each aligned block of 64 rows (the rows of one index of epouter) no expert is named by more than 48 rows, and in some block one expert is named by exactly 48 rows.
All inputs are finite; a program needn't handle non-finite values.
Results may differ from a plain program's by a relative error of at most 0.0058.
Values may be sent and summed in bfloat16 or wider, within the bound.
A program may use at most 64 MiB of HBM per device.

v0:
```python
import functools

import jax
import jax.numpy as jnp
from jax import lax
from jax.experimental import pallas as pl
from jax.experimental.pallas import tpu as pltpu
from jax.sharding import PartitionSpec as P

SLICES = 4
MESH = pl.DeviceIdType.MESH
F32 = jnp.float32
BF16 = jnp.bfloat16


def tile_of(width):
    return next(t for t in (512, 256, 128) if width % t == 0)


def each_tile(width, tile, body):
    @pl.loop(0, width // tile)
    def _(i):
        body(pl.ds(pl.multiple_of(i * tile, tile), tile))


def layer_kernel(
    experts, inner, slot, cuts,
    tokens, ids_t, weight_t, w_gate, w_up, w_down, out,
    w_in, w_out, outgoing, rows, own, x_send, x_recv, hidden, part, core_recv,
    y_send, y_recv, z_send, returned, mix,
    w_sem, zs, zr, ys, yr, cs, cr, xs, xr, ps, pr, qs, qr, bs, br,
):
    block, width = tokens.shape
    picks = ids_t.shape[0]
    hid = w_down.shape[1]
    here = lax.axis_index("epouter")
    expert = here // SLICES
    part_at = here % SLICES
    side = part_at % 2
    sib = part_at + 1 - 2 * side
    flip = lax.rem(part_at + 2, SLICES)
    sib_flip = lax.rem(sib + 2, SLICES)
    base = expert * SLICES
    x_at = lax.axis_index("epinner")
    piece = width // cuts
    tile = tile_of(piece)

    def at_layer(step):
        return {"epouter": lax.rem(expert + step + experts, experts) * SLICES + part_at}

    to_sib = {"epouter": base + sib}
    to_flip = {"epouter": base + flip}

    def at_inner(step):
        return {"epinner": lax.rem(x_at + step, inner)}

    loads = [
        pltpu.make_async_copy(w_gate.at[0], w_in.at[:, pl.ds(0, hid)], w_sem.at[0]),
        pltpu.make_async_copy(w_up.at[0], w_in.at[:, pl.ds(hid, hid)], w_sem.at[1]),
        pltpu.make_async_copy(w_down.at[0], w_out, w_sem.at[2]),
    ]

    barrier = pltpu.get_barrier_semaphore()
    partners = [at_layer(k) for k in range(1, experts)] + [to_sib, to_flip]
    partners += [at_inner(d) for d in range(1, inner)]
    for partner in partners:
        pl.semaphore_signal(barrier, inc=1, device_id=partner, device_id_type=MESH)

    named = lax.rem(expert + lax.broadcasted_iota(jnp.int32, (experts, block), 0), experts)
    chosen = jnp.zeros((experts, block), F32)
    coef = jnp.zeros((experts, block), F32)
    for p in range(picks):
        same = ids_t[p : p + 1, :] == named
        chosen += same.astype(F32)
        coef += jnp.where(same, weight_t[p : p + 1, :], 0.0)
    before = (
        lax.broadcasted_iota(jnp.int32, (block, block), 0)
        < lax.broadcasted_iota(jnp.int32, (block, block), 1)
    ).astype(F32)
    pos = jnp.dot(chosen.astype(BF16), before.astype(BF16), preferred_element_type=F32)
    pos = jnp.where(chosen > 0, pos, -1.0)
    slots = lax.broadcasted_iota(jnp.int32, (slot, block), 0).astype(F32)

    def gather_into(k, target):
        place = jnp.where(pos[k : k + 1, :] == slots, 1.0, 0.0).astype(BF16)
        for h in range(cuts):
            for j in range(piece // tile):
                at = h * piece + j * tile
                target[h, :, j * tile : (j + 1) * tile] = jnp.dot(
                    place, tokens[:, at : at + tile], preferred_element_type=F32
                ).astype(BF16)

    def remote(src, dst, send, recv, device):
        return pltpu.make_async_remote_copy(
            src_ref=src, dst_ref=dst, send_sem=send, recv_sem=recv,
            device_id=device, device_id_type=MESH,
        )

    def z_out(k, h):
        return remote(
            outgoing.at[k - 1, h], rows.at[k, part_at, h], zs.at[k, h], zr.at[k, h], at_layer(k)
        )

    def y_out(k, h):
        mine = rows.at[k, part_at, h]
        return remote(mine, mine, ys.at[k, h], yr.at[k, h], to_flip)

    def core_out(k, which, h):
        ref = rows.at[k, part_at if which == 0 else flip, h]
        return remote(ref, ref, cs.at[k, which, h], cr.at[k, which, h], to_sib)

    def x_out(k, d):
        return remote(
            x_send.at[k], x_recv.at[k, d - 1], xs.at[k, d - 1], xr.at[k, d - 1], at_inner(d)
        )

    def core_back(k, which, h):
        return remote(
            part.at[k, sib if which == 0 else sib_flip, h], core_recv.at[k, which, h],
            ps.at[k, which, h], pr.at[k, which, h], to_sib,
        )

    def y_back(k, h):
        return remote(y_send.at[k, h], y_recv.at[k, h], qs.at[k, h], qr.at[k, h], to_flip)

    def z_back(k, h):
        return remote(
            z_send.at[k - 1, h], returned.at[k, h], bs.at[k, h], br.at[k, h], at_layer(-k)
        )

    gather_into(0, rows.at[0, part_at])
    pl.semaphore_wait(barrier, len(partners))
    for h in range(cuts):
        y_out(0, h).start()
        core_out(0, 0, h).start()
    for k in range(1, experts):
        gather_into(k, outgoing.at[k - 1])
        for h in range(cuts):
            z_out(k, h).start()
    for load in loads:
        load.start()
    for k in range(experts):
        spread = jnp.where(pos[k : k + 1, :] == slots, coef[k : k + 1, :], 0.0)
        high = spread.astype(BF16).astype(F32)
        mix[k * slot : (k + 1) * slot, :] = jnp.concatenate([high, spread - high], axis=1)

    def arrive(k, h):
        if k >= experts:
            return
        z_out(k, h).wait_recv()
        y_out(k, h).start()
        core_out(k, 0, h).start()

    def forward(k, h):
        if k >= experts:
            return
        y_out(k, h).wait_recv()
        core_out(k, 1, h).start()

    def up(k):
        if k >= experts:
            return
        if k == 0:
            loads[0].wait()
            loads[1].wait()
        for h in range(cuts):
            core_out(k, 0, h).wait_recv()
            core_out(k, 1, h).wait_recv()

        def body(cols):
            value = jnp.zeros((SLICES * slot, cols.size), F32)
            for h in range(cuts):
                x = rows[k, :, h].reshape(SLICES * slot, piece)
                value += jnp.dot(
                    x, w_in[h * piece : (h + 1) * piece, cols], preferred_element_type=F32
                )
            own[k, :, cols] = value
            x_send[k, :, cols] = value.astype(BF16)

        each_tile(2 * hid, 256 if (2 * hid) % 256 == 0 else 128, body)
        for d in range(1, inner):
            x_out(k, d).start()

    def down(k):
        if not 0 <= k < experts:
            return
        for d in range(1, inner):
            x_out(k, d).wait_recv()
        if k == 0:
            loads[2].wait()

        def act(cols):
            upper = pl.ds(pl.multiple_of(cols.start + hid, 128), cols.size)
            gate = own[k, :, cols]
            lift = own[k, :, upper]
            for d in range(inner - 1):
                gate += x_recv[k, d, :, cols].astype(F32)
                lift += x_recv[k, d, :, upper].astype(F32)
            hidden[:, cols] = (gate / (1.0 + jnp.exp(-gate)) * lift).astype(BF16)

        each_tile(hid, 128, act)
        for h in range(cuts):

            def body(cols):
                above = pl.ds(pl.multiple_of(cols.start + h * piece, 128), cols.size)
                value = jnp.dot(hidden[...], w_out[:, above], preferred_element_type=F32)
                part[k, :, h, :, cols] = value.astype(BF16).reshape(SLICES, slot, tile)

            each_tile(piece, tile, body)
            core_back(k, 1, h).start()
            core_back(k, 0, h).start()

    def fold_core(k):
        if not 0 <= k < experts:
            return
        for h in range(cuts):
            core_back(k, 1, h).wait_recv()

            def body(cols):
                y_send[k, h, :, cols] = (
                    part[k, flip, h, :, cols].astype(F32)
                    + core_recv[k, 1, h, :, cols].astype(F32)
                ).astype(BF16)

            each_tile(piece, tile, body)
            y_back(k, h).start()

    def fold_y(k):
        if not 0 <= k < experts:
            return
        for h in range(cuts):
            core_back(k, 0, h).wait_recv()
            y_back(k, h).wait_recv()
            target = returned.at[0, h] if k == 0 else z_send.at[k - 1, h]

            def body(cols):
                target[:, cols] = (
                    part[k, part_at, h, :, cols].astype(F32)
                    + core_recv[k, 0, h, :, cols].astype(F32)
                    + y_recv[k, h, :, cols].astype(F32)
                ).astype(BF16)

            each_tile(piece, tile, body)
            if k:
                z_back(k, h).start()

    for t in range(experts + 1):
        for h in range(cuts):
            arrive(t + 1, h)
            forward(t, h)
        up(t)
        if t > 2:
            fold_core(t - 2)
        if t > 3:
            fold_y(t - 3)
        down(t - 1)
    if experts > 1:
        fold_core(experts - 1)
    fold_core(0)
    for k in range(max(experts - 2, 1), experts):
        fold_y(k)
    fold_y(0)

    mixed = mix[...].T.astype(BF16)
    for h in range(cuts):
        for k in range(1, experts):
            z_back(k, h).wait_recv()

        def finish(cols):
            back = returned[:, h, :, cols].reshape(experts * slot, tile)
            both = jnp.dot(mixed, back, preferred_element_type=F32)
            above = pl.ds(pl.multiple_of(cols.start + h * piece, 128), cols.size)
            out[:, above] = (both[:block] + both[block:]).astype(BF16)

        each_tile(piece, tile, finish)

    for k in range(experts):
        for h in range(cuts):
            if k:
                z_out(k, h).wait_send()
                z_back(k, h).wait_send()
            y_out(k, h).wait_send()
            y_back(k, h).wait_send()
            for which in range(2):
                core_out(k, which, h).wait_send()
                core_back(k, which, h).wait_send()
        for d in range(1, inner):
            x_out(k, d).wait_send()


def shards(tokens, expert_ids, route_weight, w_gate, w_up, w_down):
    experts = lax.axis_size("epouter") // SLICES
    inner = lax.axis_size("epinner")
    block, width = tokens.shape
    picks = expert_ids.shape[1]
    hid = w_down.shape[1]
    depth = min(block, 3 * block * picks // (2 * experts))
    slot = -(-depth // 16) * 16
    rows = SLICES * slot
    vmem = pl.BlockSpec(memory_space=pltpu.VMEM)
    hbm = pl.BlockSpec(memory_space=pl.ANY)
    dma = pltpu.SemaphoreType.DMA
    others = max(inner - 1, 1)
    away = max(experts - 1, 1)
    total = experts * rows
    cuts = 1
    piece = width // cuts
    return pl.pallas_call(
        functools.partial(layer_kernel, experts, inner, slot, cuts),
        out_shape=jax.ShapeDtypeStruct((block, width), BF16),
        in_specs=[vmem] * 3 + [hbm] * 3,
        out_specs=vmem,
        scratch_shapes=[
            pltpu.VMEM((width, 2 * hid), BF16),
            pltpu.VMEM((hid, width), BF16),
            pltpu.VMEM((away, cuts, slot, piece), BF16),
            pltpu.VMEM((experts, SLICES, cuts, slot, piece), BF16),
            pltpu.VMEM((experts, rows, 2 * hid), F32),
            pltpu.VMEM((experts, rows, 2 * hid), BF16),
            pltpu.VMEM((experts, others, rows, 2 * hid), BF16),
            pltpu.VMEM((rows, hid), BF16),
            pltpu.VMEM((experts, SLICES, cuts, slot, piece), BF16),
            pltpu.VMEM((experts, 2, cuts, slot, piece), BF16),
            pltpu.VMEM((experts, cuts, slot, piece), BF16),
            pltpu.VMEM((experts, cuts, slot, piece), BF16),
            pltpu.VMEM((away, cuts, slot, piece), BF16),
            pltpu.VMEM((experts, cuts, slot, piece), BF16),
            pltpu.VMEM((experts * slot, 2 * block), F32),
            dma((3,)),
            dma((experts, cuts)), dma((experts, cuts)),
            dma((experts, cuts)), dma((experts, cuts)),
            dma((experts, 2, cuts)), dma((experts, 2, cuts)),
            dma((experts, others)), dma((experts, others)),
            dma((experts, 2, cuts)), dma((experts, 2, cuts)),
            dma((experts, cuts)), dma((experts, cuts)),
            dma((experts, cuts)), dma((experts, cuts)),
        ],
        compiler_params=pltpu.CompilerParams(
            collective_id=0, has_side_effects=True, vmem_limit_bytes=52 * 2**20
        ),
        cost_estimate=pl.CostEstimate(
            flops=6 * total * width * hid,
            bytes_accessed=6 * width * hid + 4 * block * width,
            transcendentals=total * hid,
        ),
    )(tokens, expert_ids.T, route_weight.T, w_gate, w_up, w_down)


def solution(mesh):
    placed = (
        P(("groups", "epouter"), "epinner"),
        P(("groups", "epouter"), None),
        P(("groups", "epouter"), None),
        P("epouter", "epinner", None),
        P("epouter", "epinner", None),
        P("epouter", None, "epinner"),
    )
    return jax.shard_map(
        shards,
        mesh=mesh,
        in_specs=placed,
        out_specs=P(("groups", "epouter"), "epinner"),
        check_vma=False,
    )
```

profile of v0, /device:TPU:0, one launch (start us, length us, event | category | flops | bytes accessed | tf_op | source)
XLA Modules:
  0.0 99.2 jit_solution(15289631173210259569)
XLA Ops:
  0.0 0.0 copy-start
  0.0 1.0 %copy-done = bf16[64,3584]{1,0:T(8,128)(2,1)S(1)} copy-done((bf16[64,3584]{1,0:T(8,128)(2,1)S(1)}, bf16[64,3584]{1,0:T(8,128)(2,1)}, u32[]{:S(2)}) %copy-start) | copy-done | bytes 458776
  1.0 0.0 copy-start.1
  1.0 0.7 copy-done.1
  1.7 0.0 copy-start.2
  1.7 0.7 copy-done.2
  2.4 96.1 %shard_map.64 = bf16[64,3584]{1,0:T(8,128)(2,1)S(1)} custom-call(bf16[64,3584]{1,0:T(8,128)(2,1)S(1)} %copy-done, s32[2,64]{1,0:T(2,128)S(1)} %bitcast.2, f32[2,64]{1,0:T(2,128)S(1)} %bitcast.3, bf16[1,3584,384]{2,1,0:T(8,128)(2,1)} %w_gate.1, bf16[1,3584,384]{2,1,0:T(8,128)(2,1)} %w_up.1, bf16[1,384,3584]{2,1,0:T(8,128)(2,1)} %w_down.1), custom_call_target="tpu_custom_call" | custom-call | flops 6341787648 | bytes 9175040 | tf_op jit(solution)/shard_map/pallas_call | solution.py:308
  98.5 0.8 copy.8
Async XLA Ops:
  0.0 1.0 %copy-start = (bf16[64,3584]{1,0:T(8,128)(2,1)S(1)}, bf16[64,3584]{1,0:T(8,128)(2,1)}, u32[]{:S(2)}) copy-start(bf16[64,3584]{1,0:T(8,128)(2,1)} %tokens.1) | copy-start | bytes 1376260
  1.0 0.7 copy-start.1
  1.7 0.7 copy-start.2
where the time goes:
time: 99.4 us; the launch traced here: 99.2 us
  Pallas kernels  96.1 us (97%)
  local copies, waits for them, and re-layouts  3.14 us (3%)
    pallas_call x1, Pallas kernels, shards(): pl.pallas_call(functools.partial(layer_kernel, experts, inner, slot, cuts...  96.1 us
    unnamed x7, local copies, waits for them, and re-layouts  3.14 us

commit v1 on v0

--- a/solution.py
+++ b/solution.py
@@ -249,16 +249,14 @@
             arrive(t + 1, h)
             forward(t, h)
         up(t)
+        down(t - 1)
+        if t > 1:
+            fold_core(t - 1)
         if t > 2:
-            fold_core(t - 2)
-        if t > 3:
-            fold_y(t - 3)
-        down(t - 1)
+            fold_y(t - 2)
     if experts > 1:
-        fold_core(experts - 1)
+        fold_y(experts - 1)
     fold_core(0)
-    for k in range(max(experts - 2, 1), experts):
-        fold_y(k)
     fold_y(0)
 
     mixed = mix[...].T.astype(BF16)

time: 99.4 us -> 97.8 us (0.984)
  Pallas kernels: 96.1 us -> 94.5 us
    pallas_call x1, Pallas kernels: 96.1 us -> 94.5 us  [shards(): pl.pallas_call(functools.partial(layer_kernel, experts, inner, slot, cuts...]
where the time goes in v1:
time: 97.8 us; the launch traced here: 97.6 us
  Pallas kernels  94.5 us (97%)
  local copies, waits for them, and re-layouts  3.14 us (3%)
    pallas_call x1, Pallas kernels, shards(): pl.pallas_call(functools.partial(layer_kernel, experts, inner, slot, cuts...  94.5 us
    unnamed x7, local copies, waits for them, and re-layouts  3.14 us

profile of v1, /device:TPU:0, one launch (start us, length us, event | category | flops | bytes accessed | tf_op | source)
XLA Modules:
  0.0 97.6 jit_solution(5063481209521595565)
XLA Ops:
  0.0 0.0 copy-start
  0.0 1.0 %copy-done = bf16[64,3584]{1,0:T(8,128)(2,1)S(1)} copy-done((bf16[64,3584]{1,0:T(8,128)(2,1)S(1)}, bf16[64,3584]{1,0:T(8,128)(2,1)}, u32[]{:S(2)}) %copy-start) | copy-done | bytes 458776
  1.0 0.0 copy-start.1
  1.0 0.7 copy-done.1
  1.7 0.0 copy-start.2
  1.7 0.7 copy-done.2
  2.4 94.5 %shard_map.64 = bf16[64,3584]{1,0:T(8,128)(2,1)S(1)} custom-call(bf16[64,3584]{1,0:T(8,128)(2,1)S(1)} %copy-done, s32[2,64]{1,0:T(2,128)S(1)} %bitcast.2, f32[2,64]{1,0:T(2,128)S(1)} %bitcast.3, bf16[1,3584,384]{2,1,0:T(8,128)(2,1)} %w_gate.1, bf16[1,3584,384]{2,1,0:T(8,128)(2,1)} %w_up.1, bf16[1,384,3584]{2,1,0:T(8,128)(2,1)} %w_down.1), custom_call_target="tpu_custom_call" | custom-call | flops 6341787648 | bytes 9175040 | tf_op jit(solution)/shard_map/pallas_call | solution.py:306
  96.9 0.8 copy.8
Async XLA Ops:
  0.0 1.0 %copy-start = (bf16[64,3584]{1,0:T(8,128)(2,1)S(1)}, bf16[64,3584]{1,0:T(8,128)(2,1)}, u32[]{:S(2)}) copy-start(bf16[64,3584]{1,0:T(8,128)(2,1)} %tokens.1) | copy-start | bytes 1376260
  1.0 0.7 copy-start.1
  1.7 0.7 copy-start.2
